TPU v7x, 256 devices: a whole 4x4x8 slice. The times are simulated.
256 devices in a mesh: pipe: 8 (over x, core), expert: 32 (over y, z).
Axes of the slice: x: 4, y: 4, z: 8, core: 2. Of those that a mesh axis runs over, the one named last changes fastest.
Arguments:
- upper_grad: bfloat16 [1024, 6144], P('expert', 'pipe'), may hold values from -6 to 6
- expert_ids: int32 [1024, 4], P('expert'), may hold values from 0 to 7, as said below
- slot_index: int32 [1024, 4], P('expert'), may hold values from -1 to 23, as said below
- gate_probs: float32 [1024, 4], P('expert'), may hold values from 0.05 to 0.6
- gate_pre: bfloat16 [32, 768, 1344], P('expert'), may hold values from -6 to 6
- up_pre: bfloat16 [32, 768, 1344], P('expert'), may hold values from -6 to 6
- w_gate: bfloat16 [32, 6144, 1344], P('expert', 'pipe'), may hold values from -0.078125 to 0.078125
- w_up: bfloat16 [32, 6144, 1344], P('expert', 'pipe'), may hold values from -0.078125 to 0.078125
- w_down: bfloat16 [32, 1344, 6144], P('expert', None, 'pipe'), may hold values from -0.078125 to 0.078125
- query_heads: bfloat16 [4096, 6144], P('expert', 'pipe'), may hold values from -6 to 6
- key_heads: bfloat16 [4096, 1024], P('expert', 'pipe'), may hold values from -6 to 6
- value_heads: bfloat16 [4096, 1024], P('expert', 'pipe'), may hold values from -6 to 6
- attn_out: bfloat16 [4096, 6144], P('expert', 'pipe'), may hold values from -4 to 4
- head_grad: bfloat16 [4096, 6144], P('expert', 'pipe'), may hold values from -6 to 6
Outputs:
- moe_input_grad: bfloat16 [1024, 6144], P('expert', 'pipe')
- query_grad: bfloat16 [4096, 6144], P('expert', 'pipe')
- key_grad: bfloat16 [4096, 1024], P('expert', 'pipe')
- value_grad: bfloat16 [4096, 1024], P('expert', 'pipe')
Inputs may be any that keep to these rules, and one draw needn't show every extreme that they name: `expert_ids`: each token names 4 different experts; one expert is named by every token. `slot_index`: within the 32 tokens of one index of expert, a pair's slot is its rank among that index's pairs to the same expert in order of token then choice, or -1 once that rank reaches 24; so at most 24 slots from one index to one expert, and some expert receives 24 from every index.
All inputs are finite; a program needn't handle non-finite values.
Results may differ from a plain program's by a relative error of at most 0.019.
Values may be sent and summed in bfloat16 or wider, within the bound.
A program may use at most 64 MiB of HBM per device.

v0:
```python
import jax
import jax.numpy as jnp
from jax import lax
from jax.sharding import PartitionSpec as P

EXPERTS = 8
HEAD_DIM = 128


masked_value = -1e30


def moe_part(
    upper_grad, expert_ids, slot_index, gate_probs, gate_pre, up_pre, w_gate, w_up, w_down
):
    peers = lax.axis_size("expert")
    sharing = peers // EXPERTS
    slot_count = gate_pre.shape[1]
    capacity = slot_count // peers
    kept = slot_index >= 0
    target = jnp.where(kept, expert_ids * capacity + slot_index, -1)
    matches = target[None, :, :] == jnp.arange(EXPERTS * capacity, dtype=jnp.int32)[:, None, None]
    slot_gate = jnp.sum(jnp.where(matches, gate_probs[None, :, :], 0.0), axis=(1, 2))
    table = jnp.any(matches, axis=2).astype(jnp.bfloat16)
    picked = jnp.dot(table, upper_grad, preferred_element_type=jnp.float32)
    outgoing = (picked * slot_gate[:, None]).astype(jnp.bfloat16).reshape(EXPERTS, capacity, -1)
    outgoing = jnp.repeat(outgoing, sharing, axis=0)
    arrived = lax.all_to_all(outgoing, "expert", split_axis=0, concat_axis=0, tiled=True).reshape(
        slot_count, -1
    )
    partial_value = lax.dot_general(
        arrived, w_down[0], (((1,), (1,)), ((), ())), preferred_element_type=jnp.float32
    )
    hidden_grad = lax.psum(partial_value.astype(jnp.bfloat16), "pipe").astype(jnp.float32)
    gate_val = gate_pre[0].astype(jnp.float32)
    up_val = up_pre[0].astype(jnp.float32)
    sigmoid_val = jax.nn.sigmoid(gate_val)
    gate_grad = (
        hidden_grad * up_val * sigmoid_val * (1.0 + gate_val * (1.0 - sigmoid_val))
    ).astype(jnp.bfloat16)
    up_grad = (hidden_grad * gate_val * sigmoid_val).astype(jnp.bfloat16)
    slot_terms = lax.dot_general(
        gate_grad, w_gate[0], (((1,), (1,)), ((), ())), preferred_element_type=jnp.float32
    )
    slot_terms = slot_terms + lax.dot_general(
        up_grad, w_up[0], (((1,), (1,)), ((), ())), preferred_element_type=jnp.float32
    )
    returned = lax.all_to_all(
        slot_terms.reshape(peers, capacity, -1).astype(jnp.bfloat16),
        "expert",
        split_axis=0,
        concat_axis=0,
        tiled=True,
    ).astype(jnp.float32)
    returned = jnp.sum(returned.reshape(EXPERTS, sharing, capacity, -1), axis=1).reshape(
        EXPERTS * capacity, -1
    )
    combined = lax.dot_general(
        table.astype(jnp.float32),
        returned,
        (((0,), (0,)), ((), ())),
        precision=lax.Precision.HIGHEST,
        preferred_element_type=jnp.float32,
    )
    return (upper_grad.astype(jnp.float32) + combined).astype(jnp.bfloat16)


def attention_part(query_heads, key_heads, value_heads, attn_out, head_grad):
    key_all, value_all = (
        lax.all_gather(key_heads, "expert", axis=0, tiled=True),
        lax.all_gather(value_heads, "expert", axis=0, tiled=True),
    )
    tok_rows = query_heads.shape[0]
    seq_total = key_all.shape[0]
    group_size = query_heads.shape[1] // key_all.shape[1]
    row_count = group_size * tok_rows
    softmax_scale = HEAD_DIM ** (-0.5)
    block_len = min(256, seq_total)
    device_pos = lax.axis_index("expert")
    reach = ((device_pos + 1) * tok_rows + block_len - 1) // block_len
    row_pos = device_pos * tok_rows + jnp.tile(jnp.arange(tok_rows, dtype=jnp.int32), group_size)
    block_iota = jnp.arange(block_len, dtype=jnp.int32)

    def head_rows(matrix):
        picked_cols = matrix.reshape(tok_rows, group_size, HEAD_DIM)
        return picked_cols.transpose(1, 0, 2).reshape(row_count, HEAD_DIM)

    query_rows = head_rows(query_heads)
    grad_rows = head_rows(head_grad)
    out_rows = head_rows(attn_out)
    row_delta = jnp.sum(grad_rows.astype(jnp.float32) * out_rows.astype(jnp.float32), axis=1)

    def block_scores(block_id):
        key_block = lax.dynamic_slice_in_dim(key_all, block_id * block_len, block_len, 0)
        scores = (
            lax.dot_general(
                query_rows, key_block, (((1,), (1,)), ((), ())), preferred_element_type=jnp.float32
            )
            * softmax_scale
        )
        key_pos = block_id * block_len + block_iota
        scores = jnp.where(key_pos[None, :] <= row_pos[:, None], scores, masked_value)
        return (scores, key_block)

    def stats_step(block_id, carry):
        run_max, run_sum = carry
        scores, unused_block = block_scores(block_id)
        new_max = jnp.maximum(run_max, jnp.max(scores, axis=1))
        run_sum = run_sum * jnp.exp(run_max - new_max) + jnp.sum(
            jnp.exp(scores - new_max[:, None]), axis=1
        )
        return (new_max, run_sum)

    start_max = jnp.full((row_count,), masked_value, jnp.float32)
    start_sum = jnp.zeros((row_count,), jnp.float32)
    run_max, run_sum = lax.fori_loop(0, reach, stats_step, (start_max, start_sum))
    log_total = run_max + jnp.log(run_sum)

    def grad_step(block_id, carry):
        query_acc, key_acc, value_acc = carry
        scores, key_block = block_scores(block_id)
        value_block = lax.dynamic_slice_in_dim(value_all, block_id * block_len, block_len, 0)
        probs = jnp.exp(scores - log_total[:, None])
        probs_low = probs.astype(jnp.bfloat16)
        grad_probs = lax.dot_general(
            grad_rows, value_block, (((1,), (1,)), ((), ())), preferred_element_type=jnp.float32
        )
        grad_scores = (probs * (grad_probs - row_delta[:, None]) * softmax_scale).astype(
            jnp.bfloat16
        )
        query_acc = query_acc + jnp.dot(grad_scores, key_block, preferred_element_type=jnp.float32)
        key_block_grad = lax.dot_general(
            grad_scores, query_rows, (((0,), (0,)), ((), ())), preferred_element_type=jnp.float32
        )
        value_block_grad = lax.dot_general(
            probs_low, grad_rows, (((0,), (0,)), ((), ())), preferred_element_type=jnp.float32
        )
        key_acc = lax.dynamic_update_slice_in_dim(key_acc, key_block_grad, block_id * block_len, 0)
        value_acc = lax.dynamic_update_slice_in_dim(
            value_acc, value_block_grad, block_id * block_len, 0
        )
        return (query_acc, key_acc, value_acc)

    start_query = jnp.zeros((row_count, HEAD_DIM), jnp.float32)
    start_keys = jnp.zeros((seq_total, HEAD_DIM), jnp.float32)
    start_values = jnp.zeros((seq_total, HEAD_DIM), jnp.float32)
    query_acc, key_acc, value_acc = lax.fori_loop(
        0, reach, grad_step, (start_query, start_keys, start_values)
    )
    query_parts = (
        query_acc.reshape(group_size, tok_rows, HEAD_DIM)
        .transpose(1, 0, 2)
        .reshape(tok_rows, group_size * HEAD_DIM)
    )
    query_grad = query_parts.astype(jnp.bfloat16)
    key_sum, value_sum = (
        lax.psum_scatter(
            key_acc.astype(jnp.bfloat16), "expert", scatter_dimension=0, tiled=True
        ).astype(jnp.float32),
        lax.psum_scatter(
            value_acc.astype(jnp.bfloat16), "expert", scatter_dimension=0, tiled=True
        ).astype(jnp.float32),
    )
    return (query_grad, key_sum.astype(jnp.bfloat16), value_sum.astype(jnp.bfloat16))


def on_device(
    upper_grad,
    expert_ids,
    slot_index,
    gate_probs,
    gate_pre,
    up_pre,
    w_gate,
    w_up,
    w_down,
    query_heads,
    key_heads,
    value_heads,
    attn_out,
    head_grad,
):
    moe_grad = moe_part(
        upper_grad, expert_ids, slot_index, gate_probs, gate_pre, up_pre, w_gate, w_up, w_down
    )
    query_grad, key_grad, value_grad = attention_part(
        query_heads, key_heads, value_heads, attn_out, head_grad
    )
    return (moe_grad, query_grad, key_grad, value_grad)


def solution(mesh):
    return jax.shard_map(
        on_device,
        mesh=mesh,
        in_specs=(
            P("expert", "pipe"),
            P("expert", None),
            P("expert", None),
            P("expert", None),
            P("expert", None, None),
            P("expert", None, None),
            P("expert", "pipe", None),
            P("expert", "pipe", None),
            P("expert", None, "pipe"),
            P("expert", "pipe"),
            P("expert", "pipe"),
            P("expert", "pipe"),
            P("expert", "pipe"),
            P("expert", "pipe"),
        ),
        out_specs=(
            P("expert", "pipe"),
            P("expert", "pipe"),
            P("expert", "pipe"),
            P("expert", "pipe"),
        ),
        check_vma=False,
    )
```

profile of v0, /device:TPU:17, one launch (start us, length us, event | category | flops | bytes accessed | tf_op | source)
XLA Modules:
  0.0 688.0 jit_solution(8753452308657826523)
XLA Ops:
  10.4 1.1 fusion.48
  12.6 11.2 %all-to-all-start = ((bf16[32,24,768]{2,1,0:T(8,128)(2,1)}), bf16[32,24,768]{2,1,0:T(8,128)(2,1)}, u32[]{:S(2)}, u32[]{:S(2)}) async-start(bf16[32,24,768]{2,1,0:T(8,128)(2,1)} %bitcast.1), calls=%async_computation | async-start | bytes 2359296 | tf_op jit(solution)/shard_map/all_to_all | solution.py:28
  25.6 60.6 %all-gather.3.cloned.1.call-done = bf16[4096,128]{1,0:T(8,128)(2,1)} async-done(((bf16[128,128]{1,0:T(8,128)(2,1)}), bf16[4096,128]{1,0:T(8,128)(2,1)}) %all-gather.3.cloned.1.call-update) | async-done | bytes 1048592 | tf_op jit(solution)/shard_map/all_gather | solution.py:70
  86.2 12.2 %while.28 = (s32[]{:T(128)}, f32[768]{0:T(1024)S(1)}, f32[768]{0:T(1024)S(1)}, s32[]{:T(128)}, bf16[4096,128]{1,0:T(8,128)(2,1)}, /*index=5*/bf16[768,128]{1,0:T...) while((s32[]{:T(128)}, f32[768]{0:T(1024)S(1)}, ...), condition=%wide.region_7.8_spmd.clone, body=%wide.region_4.7_spmd.clone.sunk | while | flops 51513860 | bytes 1883303 | solution.py:116
  86.2 1.1 fusion.83
  87.5 1.1 fusion.83
  88.9 1.1 fusion.83
  90.2 1.1 fusion.83
  91.6 1.1 fusion.83
  92.9 1.1 fusion.83
  94.3 1.1 fusion.83
  95.7 1.1 fusion.83
  97.0 1.1 fusion.83
  98.4 4.4 convolution_convert_fusion
  102.8 59.9 %all-gather.5.cloned.1.call-done = bf16[4096,128]{1,0:T(8,128)(2,1)} async-done(((bf16[128,128]{1,0:T(8,128)(2,1)}), bf16[4096,128]{1,0:T(8,128)(2,1)}) %all-gather.5.cloned.1.call-update) | async-done | bytes 1048592 | tf_op jit(solution)/shard_map/all_gather | solution.py:71
  164.9 47.3 %while.29 = (s32[]{:T(128)}, f32[768,128]{1,0:T(8,128)S(1)}, bf16[4096,128]{1,0:T(8,128)(2,1)}, bf16[4096,128]{1,0:T(8,128)(2,1)}, s32[]{:T(128)}, /*index=5*/bf...) while((s32[]{:T(128)}, f32[768,128]{1,0:T(8,128)S(1)}, ...), condition=%wide.region_10.11_spmd.clone, body=%wide.region_9.10_spmd.clone.sunk | while | flops 253527040 | bytes 5585119 | solution.py:147
  164.9 1.2 fusion.94
  166.1 1.1 fusion.95
  169.0 1.2 convolution_add_fusion.3
  170.2 1.2 fusion.94
  171.4 1.1 fusion.95
  174.2 1.2 convolution_add_fusion.3
  175.5 1.2 fusion.94
  179.5 1.2 convolution_add_fusion.3
  180.7 1.2 fusion.94
  181.9 1.1 fusion.95
  184.8 1.2 convolution_add_fusion.3
  186.0 1.2 fusion.94
  187.1 1.1 fusion.95
  190.0 1.2 convolution_add_fusion.3
  191.2 1.2 fusion.94
  192.4 1.1 fusion.95
  195.3 1.2 convolution_add_fusion.3
  196.5 1.2 fusion.94
  200.5 1.2 convolution_add_fusion.3
  201.7 1.2 fusion.94
  202.9 1.1 fusion.95
  205.8 1.2 convolution_add_fusion.3
  207.0 1.2 fusion.94
  208.2 1.1 fusion.95
  211.1 1.2 convolution_add_fusion.3
  212.3 6.7 fusion.38
  219.1 3.7 add_convert_fusion
  222.7 42.9 %all-to-all-start.1 = ((bf16[32,24,768]{2,1,0:T(8,128)(2,1)}), bf16[32,24,768]{2,1,0:T(8,128)(2,1)}, u32[]{:S(2)}, u32[]{:S(2)}) async-start(bf16[32,24,768]{2,1,0:T(8,128)(2,1)} %bitcast.115), calls=%async_computation.1 | async-start | bytes 2359296 | tf_op jit(solution)/shard_map/all_to_all | solution.py:48
  267.2 21.6 %all-to-all-done.1 = bf16[32,24,768]{2,1,0:T(8,128)(2,1)} async-done(((bf16[32,24,768]{2,1,0:T(8,128)(2,1)}), bf16[32,24,768]{2,1,0:T(8,128)(2,1)}, u32[]{:S(2)}, u32[]{:S(2)}) %all-to-all-start.1) | async-done | bytes 1179680 | tf_op jit(solution)/shard_map/all_to_all | solution.py:48
  288.8 1.5 convert_reduce_fusion
  291.3 172.7 %reduce-scatter.3.cloned.1.call-done = bf16[128,128]{1,0:T(8,128)(2,1)} async-done(((bf16[4096,128]{1,0:T(8,128)(2,1)}), bf16[128,128]{1,0:T(8,128)(2,1)}) %reduce-scatter.3.cloned.1.call-update) | async-done | bytes 32784 | tf_op jit(solution)/shard_map/reduce_scatter | solution.py:157
  464.0 216.9 %reduce-scatter.5.cloned.1.call-done = bf16[128,128]{1,0:T(8,128)(2,1)} async-done(((bf16[4096,128]{1,0:T(8,128)(2,1)}), bf16[128,128]{1,0:T(8,128)(2,1)}) %reduce-scatter.5.cloned.1.call-update) | async-done | bytes 32784 | tf_op jit(solution)/shard_map/reduce_scatter | solution.py:160
  (140 shorter events, 29.5 us)
Async XLA Ops:
  8.0 90.4 %copy-start = (bf16[1,1344,768]{2,1,0:T(8,128)(2,1)S(1)}, bf16[1,1344,768]{2,1,0:T(8,128)(2,1)}, u32[]{:S(2)}) copy-start(bf16[1,1344,768]{2,1,0:T(8,128)(2,1)} %param.26) | copy-start | bytes 6193156
  8.0 78.1 %all-gather.3.cloned.1.call-start = ((), (), s32[]{:S(2)}) async-start(), calls=%async_computation.5 | async-start | bytes 1081344 | tf_op jit(solution)/shard_map/all_gather | solution.py:70
  10.3 14.3 %copy-start.1 = (bf16[128,768]{1,0:T(8,128)(2,1)S(1)}, bf16[128,768]{1,0:T(8,128)(2,1)}, u32[]{:S(2)}) copy-start(bf16[128,768]{1,0:T(8,128)(2,1)} %param.27) | copy-start | bytes 589828
  11.5 13.5 %copy-start.2 = (bf16[128,768]{1,0:T(8,128)(2,1)S(1)}, bf16[128,768]{1,0:T(8,128)(2,1)}, u32[]{:S(2)}) copy-start(bf16[128,768]{1,0:T(8,128)(2,1)} %param.31) | copy-start | bytes 589828
  12.6 12.6 %copy-start.3 = (bf16[128,768]{1,0:T(8,128)(2,1)S(1)}, bf16[128,768]{1,0:T(8,128)(2,1)}, u32[]{:S(2)}) copy-start(bf16[128,768]{1,0:T(8,128)(2,1)} %param.30) | copy-start | bytes 589828
  12.6 85.7 %all-to-all-start = ((bf16[32,24,768]{2,1,0:T(8,128)(2,1)}), bf16[32,24,768]{2,1,0:T(8,128)(2,1)}, u32[]{:S(2)}, u32[]{:S(2)}) async-start(bf16[32,24,768]{2,1,0:T(8,128)(2,1)} %bitcast.1), calls=%async_computation | async-start | bytes 2359296 | tf_op jit(solution)/shard_map/all_to_all | solution.py:28
  23.8 138.9 %all-gather.5.cloned.1.call-start = ((), (), s32[]{:S(2)}) async-start(), calls=%async_computation.6 | async-start | bytes 1081344 | tf_op jit(solution)/shard_map/all_gather | solution.py:71
  24.6 187.7 %all-reduce.2.cloned.1.call-start = ((), (), s32[]{:S(2)}) async-start(), calls=%async_computation.4 | async-start | bytes 4128768 | tf_op jit(solution)/shard_map/psum | solution.py:34
  102.8 361.2 %reduce-scatter.3.cloned.1.call-start = ((), (), s32[]{:S(2)}) async-start(), calls=%async_computation.7 | async-start | bytes 1081344 | tf_op jit(solution)/shard_map/reduce_scatter | solution.py:157
  212.3 6.8 copy-start.5
  212.3 6.8 copy-start.6
  212.3 6.8 copy-start.7
  222.7 66.1 %all-to-all-start.1 = ((bf16[32,24,768]{2,1,0:T(8,128)(2,1)}), bf16[32,24,768]{2,1,0:T(8,128)(2,1)}, u32[]{:S(2)}, u32[]{:S(2)}) async-start(bf16[32,24,768]{2,1,0:T(8,128)(2,1)} %bitcast.115), calls=%async_computation.1 | async-start | bytes 2359296 | tf_op jit(solution)/shard_map/all_to_all | solution.py:48
  265.6 415.3 %reduce-scatter.5.cloned.1.call-start = ((), (), s32[]{:S(2)}) async-start(), calls=%async_computation.8 | async-start | bytes 1081344 | tf_op jit(solution)/shard_map/reduce_scatter | solution.py:160
  265.7 24.7 %copy-start.4 = (bf16[32,768]{1,0:T(8,128)(2,1)S(1)}, bf16[32,768]{1,0:T(8,128)(2,1)}, u32[]{:S(2)}) copy-start(bf16[32,768]{1,0:T(8,128)(2,1)} %param.18) | copy-start | bytes 147460
Sparse Core Ops, SparseCore 0:
  11.4 74.6 all-gather.2
  88.7 73.9 all-gather.4
  212.4 251.5 reduce-scatter.2
  468.2 212.6 reduce-scatter.4
Sparse Core Ops, SparseCore 1:
  102.9 80.2 all-reduce.1
where the time goes:
time: 698 us; the launch traced here: 688 us
  waiting for transfers between devices  534 us (77%)
  matrix products  73.7 us (11%)
  starting transfers between devices  54.3 us (8%)
  between operations  15.5 us (2%)
    reduce_scatter x1, waiting for transfers between devices, attention_part(): lax.psum_scatter(value_acc.astype(jnp.bfloat16), 'expert', scatter_dimens...  217 us
    reduce_scatter x1, waiting for transfers between devices, attention_part(): lax.psum_scatter(key_acc.astype(jnp.bfloat16), 'expert', scatter_dimensio...  173 us
    all_gather x1, waiting for transfers between devices, attention_part(): lax.all_gather(key_heads, 'expert', axis=0, tiled=True)  60.6 us
    all_gather x1, waiting for transfers between devices, attention_part(): lax.all_gather(value_heads, 'expert', axis=0, tiled=True)  59.9 us
    all_to_all x1, starting transfers between devices, moe_part(): lax.all_to_all(slot_terms.reshape(peers, capacity, -1).astype(jnp.bfloat1...  42.9 us
    all_to_all x1, waiting for transfers between devices, moe_part(): lax.all_to_all(slot_terms.reshape(peers, capacity, -1).astype(jnp.bfloat1...  21.6 us
    dot_general x18, matrix products, block_scores(): lax.dot_general(query_rows, key_block, (((1,), (1,)), ((), ())), preferre...  20.6 us
  transfers between devices with their start and end apart: 7, of which 5 were waited for; matrix products, arithmetic and copies ran while one was open for 12% of the time, Pallas kernels for 0%

commit v1 on v0

v1 whole, which is shorter than its diff:
```python
import jax
import jax.numpy as jnp
from jax import lax
from jax.experimental import pallas as pl
from jax.experimental.pallas import tpu as pltpu
from jax.sharding import PartitionSpec as P

MESH = pl.DeviceIdType.MESH
F32 = jnp.float32
BF16 = jnp.bfloat16

EXPERTS = 8
HEAD_DIM = 128
GROUP = 6
TOK = 32
ATT = 128
CAP = 24
UNITS = 1344
COLS = 768
ROWS = GROUP * ATT
NX, NC, NY, NZ = 4, 2, 4, 8
PAIRS = NZ // 2
PAIR_SLOTS = 2 * CAP
ROW_SLOTS = NZ * CAP
HALF_SLOTS = ROW_SLOTS // 2
KEYS = 2 * ATT
BLOCKS = NY * PAIRS
SCALE = HEAD_DIM ** (-0.5)
MASKED = -1e30

NT = (((1,), (1,)), ((), ()))
TN = (((0,), (0,)), ((), ()))
NN = (((1,), (0,)), ((), ()))


def dot(a, b, dims):
    return lax.dot_general(a, b, dims, preferred_element_type=F32)


def kernel(
    upper_ref, ids_ref, slot_ref, prob_ref, gpre_hbm, upre_hbm, wg_hbm, wu_hbm, wd_hbm,
    q_ref, k_ref, v_ref, o_ref, do_ref,
    moe_ref, dq_ref, dk_ref, dv_ref,
    gpre, upre, wg, wu, wd, load_sem,
    upg, metag, stack, picks, tables, sbuf, arrived,
    hpart, csend, crecv, xsend, xrecv, hidg,
    tsend, trecv, zsend, zrecv, mown,
    kvg, qrows, dorows, delta, scores, mrun, lrun, dqt, dkv, drecv, dzsend, dzrecv, dtmp,
    up_s, up_r, meta_s, meta_r, kvz_s, kvz_r, kvy_s, kvy_r, sl_s, sl_r,
    core_s, core_r, xr_s, xr_r, xg_s, xg_r, cg_s, cg_r, t_s, t_r, tz_s, tz_r,
    dy_s, dy_r, dz_s, dz_r,
):
    p = lax.axis_index("pipe")
    e = lax.axis_index("expert")
    x, c = p // NC, p % NC
    y, z = e // NZ, e % NZ
    half = z // 4

    def at(xx, cc, yy, zz):
        return (xx * NC + cc, yy * NZ + zz)

    def z_dev(zz):
        return at(x, c, y, zz)

    def y_dev(yy):
        return at(x, c, yy, z)

    def x_dev(xx):
        return at(xx, c, y, z)

    core_dev = at(x, 1 - c, y, z)

    def remote(src, dst, ss, rs, dev):
        return pltpu.make_async_remote_copy(
            src_ref=src, dst_ref=dst, send_sem=ss, recv_sem=rs, device_id=dev, device_id_type=MESH
        )

    loads = [
        pltpu.make_async_copy(src.at[0], dst, load_sem.at[i])
        for i, (src, dst) in enumerate(
            ((wd_hbm, wd), (gpre_hbm, gpre), (upre_hbm, upre), (wg_hbm, wg), (wu_hbm, wu))
        )
    ]
    for load in loads:
        load.start()

    upg[z] = upper_ref[...]
    kept = slot_ref[...] >= 0
    metag[z] = jnp.zeros((TOK, 128), F32)
    metag[z, :, 0:4] = jnp.where(kept, ids_ref[...] * CAP + slot_ref[...], -1).astype(F32)
    metag[z, :, 4:8] = prob_ref[...]
    kvg[e, :, 0:128] = k_ref[...]
    kvg[e, :, 128:256] = v_ref[...]

    barrier = pltpu.get_barrier_semaphore()
    peers = (
        [z_dev((z + k) % NZ) for k in range(1, NZ)]
        + [y_dev((y + k) % NY) for k in range(1, NY)]
        + [x_dev((x + k) % NX) for k in range(1, NX)]
        + [core_dev]
    )
    for peer in peers:
        pl.semaphore_signal(barrier, inc=1, device_id=peer, device_id_type=MESH)
    pl.semaphore_wait(barrier, len(peers))

    z_order = (1, 7, 2, 6, 3, 5, 4)
    y_order = (1, 3, 2)

    def up_copy(zsrc, zdst):
        return remote(upg.at[zsrc], upg.at[zsrc], up_s.at[zdst], up_r.at[zsrc], z_dev(zdst))

    def meta_copy(zsrc, zdst):
        return remote(metag.at[zsrc], metag.at[zsrc], meta_s.at[zdst], meta_r.at[zsrc], z_dev(zdst))

    def kvz_copy(zsrc, zdst):
        blk = kvg.at[y * NZ + zsrc]
        return remote(blk, blk, kvz_s.at[zdst], kvz_r.at[zsrc], z_dev(zdst))

    for k in z_order:
        up_copy(z, (z + k) % NZ).start()
        meta_copy(z, (z + k) % NZ).start()
    for k in z_order:
        kvz_copy(z, (z + k) % NZ).start()

    for g in range(GROUP):
        cols = slice(g * 128, (g + 1) * 128)
        qrows[g * 128:(g + 1) * 128, :] = q_ref[:, cols]
        dorows[g * 128:(g + 1) * 128, :] = do_ref[:, cols]
        prod = do_ref[:, cols].astype(F32) * o_ref[:, cols].astype(F32)
        delta[:, cols] = jnp.sum(prod.T, axis=0, keepdims=True)

    col = lax.broadcasted_iota(jnp.int32, (TOK, 4 * PAIR_SLOTS), 1)
    col_y = (
        (col >= PAIR_SLOTS).astype(jnp.int32)
        + (col >= 2 * PAIR_SLOTS).astype(jnp.int32)
        + (col >= 3 * PAIR_SLOTS).astype(jnp.int32)
    )
    col_in = col - PAIR_SLOTS * col_y
    col_i = (col_in >= CAP).astype(jnp.int32)
    wanted = (2 * col_y + half) * CAP + (col_in - CAP * col_i)

    def slot_copy(yrel, pair):
        ydst = (y + yrel) % NY
        rows = pl.ds(pl.multiple_of(pair * PAIR_SLOTS, 16), PAIR_SLOTS)
        return remote(
            sbuf.at[ydst, rows], arrived.at[y, rows], sl_s.at[yrel - 1, pair], sl_r.at[yrel - 1, pair], y_dev(ydst)
        )

    for j in (0, 1, 3, 2):
        pair = (z // 2 + j) % PAIRS
        for i in range(2):
            zz = pair * 2 + i

            @pl.when(zz != z)
            def _():
                up_copy(zz, z).wait_recv()
                meta_copy(zz, z).wait_recv()

            meta = metag[zz]
            tokens = upg[zz].astype(F32)
            target = meta[:, 0:4].astype(jnp.int32)
            mine = jnp.where(col_i == i, wanted, -2)
            table = jnp.zeros((TOK, 4 * PAIR_SLOTS), F32)
            for k in range(4):
                row = (i * 4 + k) * TOK
                stack[row:row + TOK, :] = (meta[:, 4 + k:5 + k] * tokens).astype(BF16)
                hit = (target[:, k:k + 1] == mine).astype(F32)
                table = table + hit
                picks[row:row + TOK, :] = hit.astype(BF16)
            tables[pair, i * TOK:(i + 1) * TOK, :] = table.astype(BF16)
        picked = dot(picks[...], stack[...], TN).astype(BF16)
        rows = pl.ds(pl.multiple_of(pair * PAIR_SLOTS, 16), PAIR_SLOTS)
        for yy in range(NY):
            sbuf[yy, rows, :] = picked[yy * PAIR_SLOTS:(yy + 1) * PAIR_SLOTS]
        arrived[y, rows, :] = sbuf[y, rows, :]
        for yrel in y_order:
            slot_copy(yrel, pair).start()

    def kvy_copy(ysrc, yrel, zz):
        blk = kvg.at[ysrc * NZ + zz]
        return remote(blk, blk, kvy_s.at[yrel - 1, zz], kvy_r.at[yrel - 1, zz], y_dev((ysrc + yrel) % NY))

    def kv_forward(k, carry):
        zz = (z + k) % NZ

        @pl.when(k > 0)
        def _():
            kvz_copy(zz, z).wait_recv()

        for yrel in range(1, NY):

            @pl.when(y + yrel < NY)
            def _():
                kvy_copy(y, yrel, zz).start()

        return carry

    lax.fori_loop(0, NZ, kv_forward, 0)

    loads[0].wait()

    def core_copy(xx):
        return remote(csend.at[xx], crecv.at[xx], core_s.at[xx], core_r.at[xx], core_dev)

    for yrel in (0, 1, 3, 2):
        ysrc = (y - yrel + NY) % NY
        if yrel > 0:
            for pair in range(PAIRS):
                rows = pl.ds(pair * PAIR_SLOTS, PAIR_SLOTS)
                remote(
                    sbuf.at[ysrc, rows], arrived.at[ysrc, rows], sl_s.at[yrel - 1, pair], sl_r.at[yrel - 1, pair], y_dev(ysrc)
                ).wait_recv()
        part = dot(arrived[ysrc], wd[...], NT)
        hpart[ysrc, 0] = part[0:HALF_SLOTS]
        hpart[ysrc, 1] = part[HALF_SLOTS:]
        csend[ysrc] = hpart[ysrc, 1 - c].astype(BF16)
        core_copy(ysrc).start()

    def xr_copy(xrel):
        xdst = (x + xrel) % NX
        return remote(xsend.at[xdst], xrecv.at[xrel - 1], xr_s.at[xrel - 1], xr_r.at[xrel - 1], x_dev(xdst))

    for xrel in (2, 1, 3, 0):
        xx = (x + xrel) % NX
        core_copy(xx).wait_recv()
        total = hpart[xx, c] + crecv[xx].astype(F32)
        if xrel > 0:
            xsend[xx] = total.astype(BF16)
            xr_copy(xrel).start()
        else:
            hpart[xx, c] = total

    def score_block(b, masked):
        keys = kvg[pl.ds(2 * b, 2), :, 0:128].reshape(KEYS, 128)
        s = dot(keys, qrows[...], NT) * SCALE
        if masked:
            key_pos = b * KEYS + lax.broadcasted_iota(jnp.int32, (KEYS, ROWS), 0)
            row_pos = e * ATT + (lax.broadcasted_iota(jnp.int32, (KEYS, ROWS), 1) & 127)
            s = jnp.where(key_pos <= row_pos, s, MASKED)
        scores[b] = s
        mrun[...] = jnp.maximum(mrun[...], jnp.max(s.reshape(KEYS // 8, 8, ROWS), axis=0))

    def score_step(b, carry):
        score_block(b, False)
        return carry

    last = e // 2
    mrun[...] = jnp.full((8, ROWS), MASKED, F32)
    score_block(last, True)
    lax.fori_loop(y * PAIRS, last, score_step, 0)

    hsum = hpart[x, c]
    for xrel in (1, 3, 2):
        xr_copy(xrel).wait_recv()
        hsum = hsum + xrecv[xrel - 1].astype(F32)
    hidg[x, c] = hsum.astype(BF16)

    def xg_copy(xsrc, xrel):
        blk = hidg.at[xsrc, c]
        return remote(blk, blk, xg_s.at[xrel - 1], xg_r.at[xrel - 1], x_dev((xsrc + xrel) % NX))

    def cg_copy(xx, cc):
        blk = hidg.at[xx, cc]
        return remote(blk, blk, cg_s.at[xx], cg_r.at[xx], core_dev)

    for xrel in (2, 1, 3):
        xg_copy(x, xrel).start()
    cg_copy(x, c).start()

    for yrel in range(1, NY):

        @pl.when(y >= yrel)
        def _():
            ysrc = y - yrel

            def kv_wait(zz, carry):
                kvy_copy(ysrc, yrel, zz).wait_recv()
                return carry

            lax.fori_loop(0, NZ, kv_wait, 0)
            lax.fori_loop(ysrc * PAIRS, ysrc * PAIRS + PAIRS, score_step, 0)

    top = jnp.max(mrun[...], axis=0, keepdims=True)
    lrun[...] = jnp.zeros((8, ROWS), F32)

    def sum_step(b, carry):
        lrun[...] += jnp.sum(jnp.exp(scores[b] - top).reshape(KEYS // 8, 8, ROWS), axis=0)
        return carry

    lax.fori_loop(0, last + 1, sum_step, 0)
    log_total = top + jnp.log(jnp.sum(lrun[...], axis=0, keepdims=True))

    for load in loads[1:]:
        load.wait()

    def t_copy(yrel):
        ydst = (y + yrel) % NY
        return remote(tsend.at[ydst], trecv.at[:, y], t_s.at[yrel - 1], t_r.at[yrel - 1], y_dev(ydst))

    for xrel in (0, 1, 3, 2):
        xx = (x - xrel + NX) % NX
        if xrel > 0:
            xg_copy(xx, xrel).wait_recv()
            cg_copy(xx, c).start()
        cg_copy(xx, 1 - c).wait_recv()
        rows = pl.ds(pl.multiple_of(xx * ROW_SLOTS, 16), ROW_SLOTS)
        hid = hidg[xx].reshape(ROW_SLOTS, UNITS).astype(F32)
        a = gpre[rows, :].astype(F32)
        b = upre[rows, :].astype(F32)
        s = 1.0 / (1.0 + jnp.exp(-a))
        hs = hid * s
        gate_grad = (hs * b * (1.0 + a * (1.0 - s))).astype(BF16)
        up_grad = (hs * a).astype(BF16)
        terms = dot(gate_grad, wg[...], NT) + dot(up_grad, wu[...], NT)
        tsend[xx] = terms.astype(BF16).reshape(PAIRS, PAIR_SLOTS, COLS)

        @pl.when(xx == y)
        def _():
            trecv[:, y] = tsend[xx]

        for yrel in range(1, NY):

            @pl.when((y + yrel) % NY == xx)
            def _():
                t_copy(yrel).start()

    dqt[...] = jnp.zeros((128, ROWS), F32)
    row_delta = delta[...]

    def grad_block(b):
        keys = kvg[pl.ds(2 * b, 2), :, 0:128].reshape(KEYS, 128)
        values = kvg[pl.ds(2 * b, 2), :, 128:256].reshape(KEYS, 128)
        probs = jnp.exp(scores[b] - log_total)
        grad_probs = dot(values, dorows[...], NT)
        ds = (probs * (grad_probs - row_delta) * SCALE).astype(BF16)
        dqt[...] += dot(keys, ds, TN)
        dkv[pl.ds(2 * b, 2), :, 0:128] = dot(ds, qrows[...], NN).astype(BF16).reshape(2, ATT, 128)
        dkv[pl.ds(2 * b, 2), :, 128:256] = dot(probs.astype(BF16), dorows[...], NN).astype(BF16).reshape(2, ATT, 128)

    def dy_copy(yrel, ydst, blk):
        src = dkv.at[pl.ds(ydst * NZ + 2 * blk, 2)]
        return remote(src, drecv.at[yrel - 1, pl.ds(2 * blk, 2)], dy_s.at[yrel - 1, blk], dy_r.at[yrel - 1, blk], y_dev(ydst))

    for yrel in range(1, NY):

        @pl.when(y >= yrel)
        def _():
            def row_step(blk, carry):
                grad_block((y - yrel) * PAIRS + blk)
                dy_copy(yrel, y - yrel, blk).start()
                return carry

            lax.fori_loop(0, PAIRS, row_step, 0)

    def own_step(blk, carry):
        b = y * PAIRS + blk

        @pl.when(b <= last)
        def _():
            grad_block(b)

        @pl.when(b > last)
        def _():
            dkv[pl.ds(2 * b, 2)] = jnp.zeros((2, ATT, 256), BF16)

        return carry

    lax.fori_loop(0, PAIRS, own_step, 0)
    for g in range(GROUP):
        cols = slice(g * 128, (g + 1) * 128)
        dq_ref[:, cols] = dqt[:, cols].T.astype(BF16)

    for yrel in y_order:
        ysrc = (y - yrel + NY) % NY
        remote(
            tsend.at[y], trecv.at[:, ysrc], t_s.at[yrel - 1], t_r.at[yrel - 1], y_dev(ysrc)
        ).wait_recv()

    def tz_copy(zsrc, zdst):
        return remote(zsend.at[zdst], zrecv.at[zsrc], tz_s.at[zdst], tz_r.at[zsrc], z_dev(zdst))

    for j in (2, 1, 3, 0):
        pair = (z // 2 + j) % PAIRS
        tokens = dot(tables[pair], trecv[pair].reshape(ROW_SLOTS, COLS), NN)
        for i in range(2):
            zz = pair * 2 + i
            part = tokens[i * TOK:(i + 1) * TOK]

            @pl.when(zz == z)
            def _():
                mown[...] = part

            @pl.when(zz != z)
            def _():
                zsend[zz] = part.astype(BF16)
                tz_copy(z, zz).start()

    def dz_copy(zsrc, zdst):
        return remote(dzsend.at[zdst], dzrecv.at[zsrc], dz_s.at[zdst], dz_r.at[zsrc], z_dev(zdst))

    for yrel in range(1, NY):

        @pl.when(y + yrel < NY)
        def _():
            def dy_wait(blk, carry):
                dst = drecv.at[yrel - 1, pl.ds(2 * blk, 2)]
                remote(dst, dst, dy_s.at[yrel - 1, blk], dy_r.at[yrel - 1, blk], y_dev((y + yrel) % NY)).wait_recv()
                return carry

            lax.fori_loop(0, PAIRS, dy_wait, 0)

    def dz_step(k, carry):
        zz = (z + k) % NZ
        dtmp[...] = dkv[y * NZ + zz].astype(F32)
        for yrel in range(1, NY):

            @pl.when(y + yrel < NY)
            def _():
                dtmp[...] += drecv[yrel - 1, zz].astype(F32)

        @pl.when(k < NZ)
        def _():
            dzsend[zz] = dtmp[...].astype(BF16)
            dz_copy(z, zz).start()

        return carry

    lax.fori_loop(1, NZ + 1, dz_step, 0)

    acc = mown[...] + upper_ref[...].astype(F32)
    for k in z_order:
        zz = (z + k) % NZ
        tz_copy(zz, z).wait_recv()
        acc = acc + zrecv[zz].astype(F32)
    moe_ref[...] = acc.astype(BF16)

    for k in z_order:
        zz = (z + k) % NZ
        dz_copy(zz, z).wait_recv()
        dtmp[...] += dzrecv[zz].astype(F32)
    dk_ref[...] = dtmp[:, 0:128].astype(BF16)
    dv_ref[...] = dtmp[:, 128:256].astype(BF16)

    for k in z_order:
        zz = (z + k) % NZ
        up_copy(z, zz).wait_send()
        meta_copy(z, zz).wait_send()
        kvz_copy(z, zz).wait_send()
        tz_copy(z, zz).wait_send()
        dz_copy(z, zz).wait_send()
    for yrel in range(1, NY):
        for pair in range(PAIRS):
            slot_copy(yrel, pair).wait_send()
        t_copy(yrel).wait_send()

        @pl.when(y + yrel < NY)
        def _():
            def kvy_sent(zz, carry):
                kvy_copy(y, yrel, zz).wait_send()
                return carry

            lax.fori_loop(0, NZ, kvy_sent, 0)

        @pl.when(y >= yrel)
        def _():
            def dy_sent(blk, carry):
                dy_copy(yrel, y - yrel, blk).wait_send()
                return carry

            lax.fori_loop(0, PAIRS, dy_sent, 0)

    for xrel in range(1, NX):
        xr_copy(xrel).wait_send()
        xg_copy(x, xrel).wait_send()
    for xx in range(NX):
        core_copy(xx).wait_send()
        cg_copy(xx, c).wait_send()


def vmem(*shape, dtype=BF16):
    return pltpu.VMEM(shape, dtype)


def on_device(*args):
    dma = pltpu.SemaphoreType.DMA
    whole = pl.BlockSpec(memory_space=pltpu.VMEM)
    anywhere = pl.BlockSpec(memory_space=pl.ANY)
    outs = [(TOK, COLS), (ATT, COLS), (ATT, HEAD_DIM), (ATT, HEAD_DIM)]
    return pl.pallas_call(
        kernel,
        out_shape=[jax.ShapeDtypeStruct(shape, BF16) for shape in outs],
        in_specs=[whole] * 4 + [anywhere] * 5 + [whole] * 5,
        out_specs=[whole] * 4,
        scratch_shapes=[
            vmem(COLS, UNITS), vmem(COLS, UNITS), vmem(COLS, UNITS), vmem(COLS, UNITS), vmem(UNITS, COLS), dma((5,)),
            vmem(NZ, TOK, COLS), vmem(NZ, TOK, 128, dtype=F32), vmem(8 * TOK, COLS), vmem(8 * TOK, ROW_SLOTS),
            vmem(PAIRS, 2 * TOK, ROW_SLOTS), vmem(NY, ROW_SLOTS, COLS), vmem(NY, ROW_SLOTS, COLS),
            vmem(NX, NC, HALF_SLOTS, UNITS, dtype=F32), vmem(NX, HALF_SLOTS, UNITS), vmem(NX, HALF_SLOTS, UNITS),
            vmem(NX, HALF_SLOTS, UNITS), vmem(NX - 1, HALF_SLOTS, UNITS), vmem(NX, NC, HALF_SLOTS, UNITS),
            vmem(NY, PAIRS, PAIR_SLOTS, COLS), vmem(PAIRS, NY, PAIR_SLOTS, COLS),
            vmem(NZ, TOK, COLS), vmem(NZ, TOK, COLS), vmem(TOK, COLS, dtype=F32),
            vmem(NY * NZ, ATT, 256), vmem(ROWS, 128), vmem(ROWS, 128), vmem(1, ROWS, dtype=F32),
            vmem(BLOCKS, KEYS, ROWS, dtype=F32), vmem(8, ROWS, dtype=F32), vmem(8, ROWS, dtype=F32),
            vmem(128, ROWS, dtype=F32), vmem(NY * NZ, ATT, 256), vmem(NY - 1, NZ, ATT, 256),
            vmem(NZ, ATT, 256), vmem(NZ, ATT, 256), vmem(ATT, 256, dtype=F32),
            dma((NZ,)), dma((NZ,)), dma((NZ,)), dma((NZ,)), dma((NZ,)), dma((NZ,)),
            dma((NY - 1, NZ)), dma((NY - 1, NZ)), dma((NY - 1, PAIRS)), dma((NY - 1, PAIRS)),
            dma((NX,)), dma((NX,)), dma((NX - 1,)), dma((NX - 1,)), dma((NX - 1,)), dma((NX - 1,)), dma((NX,)), dma((NX,)),
            dma((NY - 1,)), dma((NY - 1,)), dma((NZ,)), dma((NZ,)),
            dma((NY - 1, PAIRS)), dma((NY - 1, PAIRS)), dma((NZ,)), dma((NZ,)),
        ],
        compiler_params=pltpu.CompilerParams(
            collective_id=0, has_side_effects=True, vmem_limit_bytes=60 * 1024 * 1024
        ),
        cost_estimate=pl.CostEstimate(flops=9_000_000_000, bytes_accessed=14_000_000, transcendentals=8_000_000),
        name="layer_grad",
    )(*args)


def solution(mesh):
    return jax.shard_map(
        on_device,
        mesh=mesh,
        in_specs=(
            P("expert", "pipe"),
            P("expert", None),
            P("expert", None),
            P("expert", None),
            P("expert", None, None),
            P("expert", None, None),
            P("expert", "pipe", None),
            P("expert", "pipe", None),
            P("expert", None, "pipe"),
            P("expert", "pipe"),
            P("expert", "pipe"),
            P("expert", "pipe"),
            P("expert", "pipe"),
            P("expert", "pipe"),
        ),
        out_specs=(
            P("expert", "pipe"),
            P("expert", "pipe"),
            P("expert", "pipe"),
            P("expert", "pipe"),
        ),
        check_vma=False,
    )
```

time: 698 us -> 158 us (0.23)
  the two profiles are of different devices: /device:TPU:17 before, /device:TPU:8 now
where the time goes in v1:
time: 158 us
  Pallas kernels  134 us (85%)
  local copies, waits for them, and re-layouts  23.3 us (15%)
    pallas_call x1, Pallas kernels, on_device(): pl.pallas_call(kernel, out_shape=[jax.ShapeDtypeStruct(shape, BF16) for s...  134 us
    unnamed x15, local copies, waits for them, and re-layouts  23.3 us

profile of v1, /device:TPU:8, one launch (start us, length us, event | category | flops | bytes accessed | tf_op | source)
XLA Modules:
  0.0 157.6 jit_solution(14415555172055544779)
XLA Ops:
  0.6 1.4 copy.18.ids_ref
  2.0 1.4 copy.19.slot_ref
  3.4 1.4 copy.20.prob_ref
  4.7 0.0 copy-start
  4.7 4.3 %copy.21.gpre_hbm = bf16[1,768,1344]{2,1,0:T(8,128)(2,1)} copy(bf16[1,768,1344]{1,2,0:T(8,128)(2,1)} %param.18) | data formatting | bytes 4128768 | tf_op args[4]
  9.0 0.0 copy-done
  9.0 2.4 %copy.22.upre_hbm = bf16[1,768,1344]{2,1,0:T(8,128)(2,1)} copy(bf16[1,768,1344]{1,2,0:T(8,128)(2,1)S(1)} %copy-done) | data formatting | bytes 4128768 | tf_op args[5]
  11.4 0.0 copy-start.1
  11.4 4.3 %copy.23.wg_hbm = bf16[1,768,1344]{2,1,0:T(8,128)(2,1)} copy(bf16[1,768,1344]{1,2,0:T(8,128)(2,1)} %param.20) | data formatting | bytes 4128768 | tf_op args[6]
  15.7 0.0 copy-done.1
  15.7 2.5 %copy.24.wu_hbm = bf16[1,768,1344]{2,1,0:T(8,128)(2,1)} copy(bf16[1,768,1344]{1,2,0:T(8,128)(2,1)S(1)} %copy-done.1) | data formatting | bytes 4128768 | tf_op args[7]
  18.2 133.6 %layer_grad.1 = (bf16[32,768]{1,0:T(8,128)(2,1)}, bf16[128,768]{1,0:T(8,128)(2,1)}, bf16[128,128]{1,0:T(8,128)(2,1)}, bf16[128,128]{1,0:T(8,128)(2,1)}) custom-call(bf16[32,768]{1,0:T(8,128)(2,1)} %upper_ref.1, s32[32,4]{1,0:T(8,128)} %copy.18.ids_ref, s32[32,4]{1,0:T(8,128)} %copy.19.slot_ref, f32[32,4]{1,0:T(8,128)} %copy.20.prob_ref, ...), custom_call_target="tpu_custom_call" | custom-call | flops 8999999488 | bytes 14000000 | tf_op jit(solution)/shard_map/layer_grad/pallas_call | solution.py:489
  151.8 1.4 copy.29
  153.3 1.6 %copy.30 = bf16[128,768]{1,0:T(8,128)(2,1)} copy(bf16[128,768]{1,0:T(8,128)(2,1)} %get-tuple-element.9) | data formatting | bytes 393216
  154.9 1.4 copy.31
  156.3 1.4 copy.32
Async XLA Ops:
  4.7 4.3 %copy-start = (bf16[1,768,1344]{1,2,0:T(8,128)(2,1)S(1)}, bf16[1,768,1344]{1,2,0:T(8,128)(2,1)}, u32[]{:S(2)}) copy-start(bf16[1,768,1344]{1,2,0:T(8,128)(2,1)} %param.19) | copy-start | bytes 6193156
  11.4 4.3 %copy-start.1 = (bf16[1,768,1344]{1,2,0:T(8,128)(2,1)S(1)}, bf16[1,768,1344]{1,2,0:T(8,128)(2,1)}, u32[]{:S(2)}) copy-start(bf16[1,768,1344]{1,2,0:T(8,128)(2,1)} %param.21) | copy-start | bytes 6193156

commit v2 on v1

v2 whole, which is shorter than its diff:
```python
import jax
import jax.numpy as jnp
from jax import lax
from jax.experimental import pallas as pl
from jax.experimental.pallas import tpu as pltpu
from jax.sharding import PartitionSpec as P

MESH = pl.DeviceIdType.MESH
F32 = jnp.float32
BF16 = jnp.bfloat16

EXPERTS = 8
HEAD_DIM = 128
GROUP = 6
TOK = 32
ATT = 128
CAP = 24
UNITS = 1344
COLS = 768
HALF_COLS = COLS // 2
ROWS = GROUP * ATT
NX, NC, NY, NZ = 4, 2, 4, 8
PAIRS = NZ // 2
PAIR_SLOTS = 2 * CAP
ROW_SLOTS = NZ * CAP
KEYS = 2 * ATT
BLOCKS = NY * PAIRS
SCALE = HEAD_DIM ** (-0.5)
MASKED = -1e30

NT = (((1,), (1,)), ((), ()))
TN = (((0,), (0,)), ((), ()))
NN = (((1,), (0,)), ((), ()))


def dot(a, b, dims):
    return lax.dot_general(a, b, dims, preferred_element_type=F32)


def kernel(
    upper_ref, ids_ref, slot_ref, prob_ref, gpre_hbm, upre_hbm, wg_hbm, wu_hbm, wd_hbm,
    q_hbm, k_hbm, v_hbm, o_hbm, do_hbm,
    moe_ref, dq_ref, dk_ref, dv_ref,
    gpre, upre, gpre_t, upre_t, wg, wu, wd, q_ref, o_ref, do_ref, load_sem,
    upg, metag, stack, picks, tables, sbuf, arrived,
    hpart, csend, crecv, xsend, xrecv, hown, hidg,
    tsend, trecv, zsend, zrecv, mown,
    kg, vg, qrows, dorows, delta, scores, mrun, lrun, stat, dqt, dkv, drecv, d2recv, d2sum, d2in, dzsend, dzrecv, dtmp, down,
    up_s, up_r, meta_s, meta_r, kvz_s, kvz_r, kvy_s, kvy_r, sl_s, sl_r,
    core_s, core_r, xr_s, xr_r, xg_s, xg_r, cg_s, cg_r, t_s, t_r, tz_s, tz_r,
    dy_s, dy_r, dz_s, dz_r, kv2y_s, kv2y_r, kv2z_s, kv2z_r, d2z_s, d2z_r, d2y_s, d2y_r,
):
    p = lax.axis_index("pipe")
    e = lax.axis_index("expert")
    x, c = p // NC, p % NC
    y, z = e // NZ, e % NZ
    half = z // 4

    def at(xx, cc, yy, zz):
        return (xx * NC + cc, yy * NZ + zz)

    def z_dev(zz):
        return at(x, c, y, zz)

    def y_dev(yy):
        return at(x, c, yy, z)

    def x_dev(xx):
        return at(xx, c, y, z)

    core_dev = at(x, 1 - c, y, z)

    def remote(src, dst, ss, rs, dev):
        return pltpu.make_async_remote_copy(
            src_ref=src, dst_ref=dst, send_sem=ss, recv_sem=rs, device_id=dev, device_id_type=MESH
        )

    loads = [
        pltpu.make_async_copy(src, dst, load_sem.at[i])
        for i, (src, dst) in enumerate(
            (
                (wd_hbm.at[0], wd), (gpre_hbm.at[0], gpre_t), (upre_hbm.at[0], upre_t), (wg_hbm.at[0], wg), (wu_hbm.at[0], wu),
                (k_hbm, kg.at[e]), (v_hbm, vg.at[e]), (q_hbm, q_ref), (o_hbm, o_ref), (do_hbm, do_ref),
            )
        )
    ]
    for n in (5, 6, 1, 2, 0, 7, 9, 8, 3, 4):
        loads[n].start()

    upg[z] = upper_ref[...]
    kept = slot_ref[...] >= 0
    dtmp[...] = jnp.zeros((ATT, 256), F32)
    dtmp[0:4, 0:TOK] = jnp.where(kept, ids_ref[...] * CAP + slot_ref[...], -1).astype(F32)
    dtmp[4:8, 0:TOK] = prob_ref[...]
    metag[z] = dtmp[:, 0:128].T[0:TOK]

    barrier = pltpu.get_barrier_semaphore()
    peers = (
        [z_dev((z + k) % NZ) for k in range(1, NZ)]
        + [y_dev((y + k) % NY) for k in range(1, NY)]
        + [x_dev((x + k) % NX) for k in range(1, NX)]
        + [core_dev]
    )
    for peer in peers:
        pl.semaphore_signal(barrier, inc=1, device_id=peer, device_id_type=MESH)
    pl.semaphore_wait(barrier, len(peers))

    z_order = (1, 7, 2, 6, 3, 5, 4)
    y_order = (1, 3, 2)

    def up_copy(zsrc, zdst):
        return remote(upg.at[zsrc], upg.at[zsrc], up_s.at[zdst], up_r.at[zsrc], z_dev(zdst))

    def meta_copy(zsrc, zdst):
        return remote(metag.at[zsrc], metag.at[zsrc], meta_s.at[zdst], meta_r.at[zsrc], z_dev(zdst))

    def kvz_needed(zsrc, zdst):
        return (y < NY - 1) | (zdst // 2 >= zsrc // 2)

    def kv2y_copy(buf, n, ysrc):
        blk = buf.at[ysrc * NZ + z]
        return remote(blk, blk, kv2y_s.at[n], kv2y_r.at[n], y_dev((ysrc + 2) % NY))

    def kv2z_copy(buf, n, zsrc, zdst):
        blk = buf.at[(y - 2) * NZ + zsrc]
        return remote(blk, blk, kv2z_s.at[n, zdst], kv2z_r.at[n, zsrc], z_dev(zdst))

    def kvz_copy(buf, n, zsrc, zdst):
        blk = buf.at[y * NZ + zsrc]
        return remote(blk, blk, kvz_s.at[n, zdst], kvz_r.at[n, zsrc], z_dev(zdst))

    for k in z_order:
        up_copy(z, (z + k) % NZ).start()
        meta_copy(z, (z + k) % NZ).start()
    col = lax.broadcasted_iota(jnp.int32, (TOK, 4 * PAIR_SLOTS), 1)
    col_y = (
        (col >= PAIR_SLOTS).astype(jnp.int32)
        + (col >= 2 * PAIR_SLOTS).astype(jnp.int32)
        + (col >= 3 * PAIR_SLOTS).astype(jnp.int32)
    )
    col_in = col - PAIR_SLOTS * col_y
    col_i = (col_in >= CAP).astype(jnp.int32)
    wanted = (2 * col_y + half) * CAP + (col_in - CAP * col_i)

    def slot_copy(yrel, pair):
        ydst = (y + yrel) % NY
        rows = pl.ds(pl.multiple_of(pair * PAIR_SLOTS, 16), PAIR_SLOTS)
        return remote(
            sbuf.at[ydst, rows], arrived.at[y, rows], sl_s.at[yrel - 1, pair], sl_r.at[yrel - 1, pair], y_dev(ydst)
        )

    sources = ((1, 2), (3, 0))

    def source_row(h, cc):
        return (y + NY - jnp.where(cc == 0, sources[h][0], sources[h][1])) % NY

    def core_copy(h):
        return remote(csend.at[h], crecv.at[h], core_s.at[h], core_r.at[h], core_dev)

    def xr_copy(h, xrel):
        xdst = (x + xrel) % NX
        return remote(
            xsend.at[h, xdst], xrecv.at[h, xrel - 1], xr_s.at[h, xrel - 1], xr_r.at[h, xrel - 1], x_dev(xdst)
        )

    def slots_wait(yrel):
        ysrc = (y - yrel + NY) % NY
        for pair in range(PAIRS):
            rows = pl.ds(pair * PAIR_SLOTS, PAIR_SLOTS)
            remote(
                sbuf.at[ysrc, rows], arrived.at[ysrc, rows], sl_s.at[yrel - 1, pair], sl_r.at[yrel - 1, pair], y_dev(ysrc)
            ).wait_recv()

    def hidden_other(h):
        csend[h] = dot(arrived[source_row(h, 1 - c)], wd[...], NT).astype(BF16)
        core_copy(h).start()

    def hidden_mine(h):
        hpart[h] = dot(arrived[source_row(h, c)], wd[...], NT)

    def hidden_sum(h):
        core_copy(h).wait_recv()
        for xrel in (2, 1, 3, 0):
            xx = (x + xrel) % NX
            rows = pl.ds(pl.multiple_of(xx * PAIR_SLOTS, 16), PAIR_SLOTS)
            total = hpart[h, rows] + crecv[h, rows].astype(F32)
            if xrel > 0:
                xsend[h, xx] = total.astype(BF16)
                xr_copy(h, xrel).start()
            else:
                hown[h] = total

    def kvy_copy(buf, n, ysrc, yrel, zz):
        blk = buf.at[ysrc * NZ + zz]
        return remote(blk, blk, kvy_s.at[n, yrel - 1, zz], kvy_r.at[n, yrel - 1, zz], y_dev((ysrc + yrel) % NY))

    def kv_on(n):
        buf = (kg, vg)[n]

        def kv_forward(k, carry):
            zz = (z + k) % NZ

            @pl.when((k > 0) & kvz_needed(zz, z))
            def _():
                kvz_copy(buf, n, zz, z).wait_recv()

            for yrel in (1, 3):

                @pl.when(y + yrel < NY)
                def _():
                    kvy_copy(buf, n, y, yrel, zz).start()

            return carry

        lax.fori_loop(0, NZ, kv_forward, 0)

    def score_block(b, masked):
        keys = kg[pl.ds(2 * b, 2)].reshape(KEYS, 128)
        s = dot(keys, qrows[...], NT) * SCALE
        if masked:
            key_pos = b * KEYS + lax.broadcasted_iota(jnp.int32, (KEYS, ROWS), 0)
            row_pos = e * ATT + (lax.broadcasted_iota(jnp.int32, (KEYS, ROWS), 1) & 127)
            s = jnp.where(key_pos <= row_pos, s, MASKED)
        scores[b] = s
        mrun[...] = jnp.maximum(mrun[...], jnp.max(s.reshape(KEYS // 8, 8, ROWS), axis=0))

    def score_step(b, carry):
        score_block(b, False)
        return carry

    last = e // 2

    def xg_copy(h, xsrc, xrel):
        blk = hidg.at[h, c, xsrc]
        return remote(blk, blk, xg_s.at[h, xrel - 1], xg_r.at[h, xrel - 1], x_dev((xsrc + xrel) % NX))

    def cg_copy(h, xx, cc):
        blk = hidg.at[h, cc, xx]
        return remote(blk, blk, cg_s.at[h, xx], cg_r.at[h, xx], core_dev)

    def t_copy(n, yrel):
        ydst = (y + yrel) % NY
        return remote(tsend.at[ydst, n], trecv.at[n, :, y], t_s.at[n, yrel - 1], t_r.at[n, yrel - 1], y_dev(ydst))

    def slot_terms(h, cc):
        ysrc = source_row(h, cc)
        rows = pl.ds(pl.multiple_of(ysrc * ROW_SLOTS, 16), ROW_SLOTS)
        hid = hidg[h, cc].reshape(ROW_SLOTS, UNITS).astype(F32)
        a = gpre[rows, :].astype(F32)
        b = upre[rows, :].astype(F32)
        s = 1.0 / (1.0 + jnp.exp(-a))
        hs = hid * s
        gate_grad = (hs * b * (1.0 + a * (1.0 - s))).astype(BF16)
        up_grad = (hs * a).astype(BF16)
        rel = (ysrc - y + NY) % NY
        for n in range(2):
            cols = slice(n * HALF_COLS, (n + 1) * HALF_COLS)
            part = dot(gate_grad, wg[:, cols], NN) + dot(up_grad, wu[:, cols], NN)
            tsend[ysrc, n] = part.astype(BF16).reshape(PAIRS, PAIR_SLOTS, HALF_COLS)

            @pl.when(rel == 0)
            def _():
                trecv[n, :, y] = tsend[y, n]

            @pl.when(rel > 0)
            def _():
                t_copy(n, rel).start()

    def grad_block(b):
        keys = kg[pl.ds(2 * b, 2)].reshape(KEYS, 128)
        values = vg[pl.ds(2 * b, 2)].reshape(KEYS, 128)
        probs = jnp.exp(scores[b] - stat[...])
        grad_probs = dot(values, dorows[...], NT)
        ds = (probs * (grad_probs - delta[...]) * SCALE).astype(BF16)
        dqt[...] += dot(keys, ds, TN)
        dkv[pl.ds(2 * b, 2), :, 0:128] = dot(ds, qrows[...], NN).astype(BF16).reshape(2, ATT, 128)
        dkv[pl.ds(2 * b, 2), :, 128:256] = dot(probs.astype(BF16), dorows[...], NN).astype(BF16).reshape(2, ATT, 128)

    def dy_copy(yrel, ydst, blk):
        src = dkv.at[pl.ds(ydst * NZ + 2 * blk, 2)]
        return remote(src, drecv.at[yrel - 1, pl.ds(2 * blk, 2)], dy_s.at[yrel - 1, blk], dy_r.at[yrel - 1, blk], y_dev(ydst))

    def d2z_copy(zsrc, zdst):
        return remote(
            dkv.at[(y - 2) * NZ + zdst], d2recv.at[zsrc], d2z_s.at[zdst], d2z_r.at[zsrc], z_dev(zdst)
        )

    def d2y_copy(ydst):
        return remote(d2sum, d2in, d2y_s.at[0], d2y_r.at[0], y_dev(ydst))

    def row_sum():
        @pl.when(y >= 2)
        def _():
            dtmp[...] = dkv[(y - 2) * NZ + z].astype(F32)
            for k in z_order:
                zz = (z + k) % NZ
                d2z_copy(zz, z).wait_recv()
                dtmp[...] += d2recv[zz].astype(F32)
            d2sum[...] = dtmp[...].astype(BF16)
            d2y_copy((y + 2) % NY).start()

    def tz_copy(n, zsrc, zdst):
        return remote(zsend.at[n, zdst], zrecv.at[n, zsrc], tz_s.at[n, zdst], tz_r.at[n, zsrc], z_dev(zdst))

    def send_kv():
        for n, buf in enumerate((kg, vg)):

            @pl.when(y < 2)
            def _():
                kv2y_copy(buf, n, y).start()

        for n, buf in enumerate((kg, vg)):
            for k in z_order:
                zdst = (z + k) % NZ

                @pl.when(kvz_needed(z, zdst))
                def _():
                    kvz_copy(buf, n, z, zdst).start()

    def kv2_on(n):
        buf = (kg, vg)[n]

        @pl.when(y >= 2)
        def _():
            kv2y_copy(buf, n, y - 2).wait_recv()
            for k in z_order:
                kv2z_copy(buf, n, z, (z + k) % NZ).start()

    def kv2_wait(n):
        for k in z_order:
            kv2z_copy((kg, vg)[n], n, (z + k) % NZ, z).wait_recv()

    def turn_gate():
        loads[1].wait()
        for i in range(COLS // 128):
            cols = slice(i * 128, (i + 1) * 128)
            gpre[cols, :] = gpre_t[:, cols].T

    def turn_up():
        loads[2].wait()
        for i in range(COLS // 128):
            cols = slice(i * 128, (i + 1) * 128)
            upre[cols, :] = upre_t[:, cols].T

    def prepare():
        for n in (7, 8, 9):
            loads[n].wait()
        for g in range(GROUP):
            cols = slice(g * 128, (g + 1) * 128)
            qrows[g * 128:(g + 1) * 128, :] = q_ref[:, cols]
            dorows[g * 128:(g + 1) * 128, :] = do_ref[:, cols]
            prod = do_ref[:, cols].astype(F32) * o_ref[:, cols].astype(F32)
            delta[:, cols] = jnp.sum(prod.T, axis=0, keepdims=True)

    def dispatch():
        for j in (0, 1, 3, 2):
            pair = (z // 2 + j) % PAIRS
            for i in range(2):
                zz = pair * 2 + i

                @pl.when(zz != z)
                def _():
                    up_copy(zz, z).wait_recv()
                    meta_copy(zz, z).wait_recv()

                meta = metag[zz]
                tokens = upg[zz].astype(F32)
                target = meta[:, 0:4].astype(jnp.int32)
                mine = jnp.where(col_i == i, wanted, -2)
                table = jnp.zeros((TOK, 4 * PAIR_SLOTS), F32)
                for k in range(4):
                    row = (i * 4 + k) * TOK
                    stack[row:row + TOK, :] = (meta[:, 4 + k:5 + k] * tokens).astype(BF16)
                    hit = (target[:, k:k + 1] == mine).astype(F32)
                    table = table + hit
                    picks[row:row + TOK, :] = hit.astype(BF16)
                tables[pair, i * TOK:(i + 1) * TOK, :] = table.astype(BF16)
            picked = dot(picks[...], stack[...], TN).astype(BF16)
            rows = pl.ds(pl.multiple_of(pair * PAIR_SLOTS, 16), PAIR_SLOTS)
            for yy in range(NY):
                sbuf[yy, rows, :] = picked[yy * PAIR_SLOTS:(yy + 1) * PAIR_SLOTS]
            arrived[y, rows, :] = sbuf[y, rows, :]
            for yrel in y_order:
                slot_copy(yrel, pair).start()

    def own_scores():
        mrun[...] = jnp.full((8, ROWS), MASKED, F32)
        score_block(last, True)
        lax.fori_loop(y * PAIRS, last, score_step, 0)

    def row_scores(yrel):
        @pl.when(y >= yrel)
        def _():
            ysrc = y - yrel

            def k_wait(zz, carry):
                kvy_copy(kg, 0, ysrc, yrel, zz).wait_recv()
                return carry

            if yrel == 2:
                kv2_wait(0)
            else:
                lax.fori_loop(0, NZ, k_wait, 0)
            lax.fori_loop(ysrc * PAIRS, ysrc * PAIRS + PAIRS, score_step, 0)

    def totals():
        top = jnp.max(mrun[...], axis=0, keepdims=True)
        lrun[...] = jnp.zeros((8, ROWS), F32)

        def sum_step(b, carry):
            lrun[...] += jnp.sum(jnp.exp(scores[b] - top).reshape(KEYS // 8, 8, ROWS), axis=0)
            return carry

        lax.fori_loop(0, last + 1, sum_step, 0)
        stat[...] = top + jnp.log(jnp.sum(lrun[...], axis=0, keepdims=True))
        dqt[...] = jnp.zeros((128, ROWS), F32)

    def gather_hidden(h):
        hsum = hown[h]
        for xrel in (1, 3, 2):
            xr_copy(h, xrel).wait_recv()
            hsum = hsum + xrecv[h, xrel - 1].astype(F32)
        hidg[h, c, x] = hsum.astype(BF16)
        for xrel in (2, 1, 3):
            xg_copy(h, x, xrel).start()
        cg_copy(h, x, c).start()

    def terms(h):
        for xrel in (1, 3, 2):
            xx = (x - xrel + NX) % NX
            xg_copy(h, xx, xrel).wait_recv()
            cg_copy(h, xx, c).start()
        slot_terms(h, c)
        for xx in range(NX):
            cg_copy(h, xx, 1 - c).wait_recv()
        slot_terms(h, 1 - c)

    def row_grads(yrel):
        @pl.when(y >= yrel)
        def _():
            def v_wait(zz, carry):
                kvy_copy(vg, 1, y - yrel, yrel, zz).wait_recv()
                return carry

            if yrel == 2:
                kv2_wait(1)
            else:
                lax.fori_loop(0, NZ, v_wait, 0)

            def row_step(turn, carry):
                blk = (z // 2 + 1 + turn) % PAIRS
                grad_block((y - yrel) * PAIRS + blk)
                if yrel == 2:
                    for i in range(2):
                        zz = 2 * blk + i

                        @pl.when(zz != z)
                        def _():
                            d2z_copy(z, zz).start()

                else:
                    dy_copy(yrel, y - yrel, blk).start()
                return carry

            lax.fori_loop(0, PAIRS, row_step, 0)

    def combine(n):
        for yrel in y_order:
            ysrc = (y - yrel + NY) % NY
            remote(
                tsend.at[y, n], trecv.at[n, :, ysrc], t_s.at[n, yrel - 1], t_r.at[n, yrel - 1], y_dev(ysrc)
            ).wait_recv()

        for j in (2, 1, 3, 0):
            pair = (z // 2 + j) % PAIRS
            tokens = dot(tables[pair], trecv[n, pair].reshape(ROW_SLOTS, HALF_COLS), NN)
            for i in range(2):
                zz = pair * 2 + i
                part = tokens[i * TOK:(i + 1) * TOK]

                @pl.when(zz == z)
                def _():
                    mown[n] = part

                @pl.when(zz != z)
                def _():
                    zsend[n, zz] = part.astype(BF16)
                    tz_copy(n, z, zz).start()

    def own_grads():
        def own_step(blk, carry):
            b = y * PAIRS + blk

            @pl.when(b <= last)
            def _():
                grad_block(b)

            @pl.when(b > last)
            def _():
                dkv[pl.ds(2 * b, 2)] = jnp.zeros((2, ATT, 256), BF16)

            return carry

        lax.fori_loop(0, PAIRS, own_step, 0)
        for g in range(GROUP):
            cols = slice(g * 128, (g + 1) * 128)
            dq_ref[:, cols] = dqt[:, cols].T.astype(BF16)

    def dz_copy(zsrc, zdst):
        return remote(dzsend.at[zdst], dzrecv.at[zsrc], dz_s.at[zdst], dz_r.at[zsrc], z_dev(zdst))

    def dz_needed(zsrc, zdst):
        return (y < NY - 1) | (zdst < zsrc)

    def spread():
        def pair_step(turn, carry):
            blk = (z // 2 + 1 + turn) % PAIRS
            for yrel in (1, 3):

                @pl.when(y + yrel < NY)
                def _():
                    dst = drecv.at[yrel - 1, pl.ds(2 * blk, 2)]
                    remote(
                        dst, dst, dy_s.at[yrel - 1, blk], dy_r.at[yrel - 1, blk], y_dev((y + yrel) % NY)
                    ).wait_recv()

            for i in range(2):
                zz = 2 * blk + (z + 1 + i) % 2
                dtmp[...] = dkv[y * NZ + zz].astype(F32)
                for yrel in (1, 3):

                    @pl.when(y + yrel < NY)
                    def _():
                        dtmp[...] += drecv[yrel - 1, zz].astype(F32)

                @pl.when((zz != z) & dz_needed(z, zz))
                def _():
                    dzsend[zz] = dtmp[...].astype(BF16)
                    dz_copy(z, zz).start()

            return carry

        lax.fori_loop(0, PAIRS, pair_step, 0)
        down[...] = dtmp[...]

    turn_gate()
    dispatch()
    for n in (5, 6):
        loads[n].wait()
    send_kv()
    turn_up()
    prepare()
    loads[0].wait()
    slots_wait(1)
    slots_wait(2)
    hidden_other(0)
    hidden_mine(0)
    slots_wait(3)
    hidden_other(1)
    hidden_sum(0)
    hidden_mine(1)
    hidden_sum(1)
    kv2_on(0)
    kv2_on(1)
    kv_on(0)
    kv_on(1)
    own_scores()
    gather_hidden(0)
    gather_hidden(1)
    for yrel in (1, 3, 2):
        row_scores(yrel)
    totals()
    loads[3].wait()
    loads[4].wait()
    terms(0)
    terms(1)
    for yrel in (2, 3, 1):
        row_grads(yrel)
    combine(0)
    combine(1)
    row_sum()
    own_grads()
    spread()

    for n in range(2):
        cols = slice(n * HALF_COLS, (n + 1) * HALF_COLS)
        acc = mown[n] + upper_ref[:, cols].astype(F32)
        for k in z_order:
            zz = (z + k) % NZ
            tz_copy(n, zz, z).wait_recv()
            acc = acc + zrecv[n, zz].astype(F32)
        moe_ref[:, cols] = acc.astype(BF16)

    for k in z_order:
        zz = (z + k) % NZ

        @pl.when(dz_needed(zz, z))
        def _():
            dz_copy(zz, z).wait_recv()
            down[...] += dzrecv[zz].astype(F32)

    @pl.when(y < 2)
    def _():
        d2y_copy(y).wait_recv()
        down[...] += d2in[...].astype(F32)

    dk_ref[...] = down[:, 0:128].astype(BF16)
    dv_ref[...] = down[:, 128:256].astype(BF16)

    for k in z_order:
        zz = (z + k) % NZ
        up_copy(z, zz).wait_send()
        meta_copy(z, zz).wait_send()
        tz_copy(0, z, zz).wait_send()
        tz_copy(1, z, zz).wait_send()

        @pl.when(kvz_needed(z, zz))
        def _():
            kvz_copy(kg, 0, z, zz).wait_send()
            kvz_copy(vg, 1, z, zz).wait_send()

        @pl.when(dz_needed(z, zz))
        def _():
            dz_copy(z, zz).wait_send()

        @pl.when(y >= 2)
        def _():
            kv2z_copy(kg, 0, z, zz).wait_send()
            kv2z_copy(vg, 1, z, zz).wait_send()
            d2z_copy(z, zz).wait_send()

    @pl.when(y >= 2)
    def _():
        d2y_copy((y + 2) % NY).wait_send()

    @pl.when(y < 2)
    def _():
        kv2y_copy(kg, 0, y).wait_send()
        kv2y_copy(vg, 1, y).wait_send()

    for yrel in range(1, NY):
        for pair in range(PAIRS):
            slot_copy(yrel, pair).wait_send()
        t_copy(0, yrel).wait_send()
        t_copy(1, yrel).wait_send()

    for yrel in (1, 3):

        @pl.when(y + yrel < NY)
        def _():
            def kvy_sent(zz, carry):
                kvy_copy(kg, 0, y, yrel, zz).wait_send()
                kvy_copy(vg, 1, y, yrel, zz).wait_send()
                return carry

            lax.fori_loop(0, NZ, kvy_sent, 0)

        @pl.when(y >= yrel)
        def _():
            def dy_sent(blk, carry):
                dy_copy(yrel, y - yrel, blk).wait_send()
                return carry

            lax.fori_loop(0, PAIRS, dy_sent, 0)

    for h in range(2):
        core_copy(h).wait_send()
        for xrel in range(1, NX):
            xr_copy(h, xrel).wait_send()
            xg_copy(h, x, xrel).wait_send()
        for xx in range(NX):
            cg_copy(h, xx, c).wait_send()


def vmem(*shape, dtype=BF16):
    return pltpu.VMEM(shape, dtype)


def copy_kernel(*refs):
    for i in range(4):
        refs[4 + i][...] = refs[i][...]


def on_device(upper, ids, slots, probs, gate_pre, up_pre, w_gate, w_up, *rest):
    args = (upper, ids.T, slots.T, probs.T) + tuple(jnp.swapaxes(a, 1, 2) for a in (gate_pre, up_pre, w_gate, w_up)) + rest
    dma = pltpu.SemaphoreType.DMA
    whole = pl.BlockSpec(memory_space=pltpu.VMEM)
    anywhere = pl.BlockSpec(memory_space=pl.ANY)
    outs = [(TOK, COLS), (ATT, COLS), (ATT, HEAD_DIM), (ATT, HEAD_DIM)]
    out_shape = [jax.ShapeDtypeStruct(shape, BF16) for shape in outs]
    grads = pl.pallas_call(
        kernel,
        out_shape=out_shape,
        in_specs=[whole] * 4 + [anywhere] * 10,
        out_specs=[whole] * 4,
        scratch_shapes=[
            vmem(COLS, UNITS), vmem(COLS, UNITS), vmem(UNITS, COLS), vmem(UNITS, COLS),
            vmem(UNITS, COLS), vmem(UNITS, COLS), vmem(UNITS, COLS), vmem(ATT, COLS), vmem(ATT, COLS), vmem(ATT, COLS), dma((10,)),
            vmem(NZ, TOK, COLS), vmem(NZ, TOK, 128, dtype=F32), vmem(8 * TOK, COLS), vmem(8 * TOK, ROW_SLOTS),
            vmem(PAIRS, 2 * TOK, ROW_SLOTS), vmem(NY, ROW_SLOTS, COLS), vmem(NY, ROW_SLOTS, COLS),
            vmem(2, ROW_SLOTS, UNITS, dtype=F32), vmem(2, ROW_SLOTS, UNITS), vmem(2, ROW_SLOTS, UNITS),
            vmem(2, NX, PAIR_SLOTS, UNITS), vmem(2, NX - 1, PAIR_SLOTS, UNITS), vmem(2, PAIR_SLOTS, UNITS, dtype=F32),
            vmem(2, NC, NX, PAIR_SLOTS, UNITS),
            vmem(NY, 2, PAIRS, PAIR_SLOTS, HALF_COLS), vmem(2, PAIRS, NY, PAIR_SLOTS, HALF_COLS),
            vmem(2, NZ, TOK, HALF_COLS), vmem(2, NZ, TOK, HALF_COLS), vmem(2, TOK, HALF_COLS, dtype=F32),
            vmem(NY * NZ, ATT, 128), vmem(NY * NZ, ATT, 128), vmem(ROWS, 128), vmem(ROWS, 128), vmem(1, ROWS, dtype=F32),
            vmem(BLOCKS, KEYS, ROWS, dtype=F32), vmem(8, ROWS, dtype=F32), vmem(8, ROWS, dtype=F32), vmem(1, ROWS, dtype=F32),
            vmem(128, ROWS, dtype=F32), vmem(NY * NZ, ATT, 256), vmem(NY - 1, NZ, ATT, 256), vmem(NZ, ATT, 256), vmem(ATT, 256), vmem(ATT, 256),
            vmem(NZ, ATT, 256), vmem(NZ, ATT, 256), vmem(ATT, 256, dtype=F32), vmem(ATT, 256, dtype=F32),
            dma((NZ,)), dma((NZ,)), dma((NZ,)), dma((NZ,)), dma((2, NZ)), dma((2, NZ)),
            dma((2, NY - 1, NZ)), dma((2, NY - 1, NZ)), dma((NY - 1, PAIRS)), dma((NY - 1, PAIRS)),
            dma((2,)), dma((2,)), dma((2, NX - 1)), dma((2, NX - 1)), dma((2, NX - 1)), dma((2, NX - 1)),
            dma((2, NX)), dma((2, NX)),
            dma((2, NY - 1)), dma((2, NY - 1)), dma((2, NZ)), dma((2, NZ)),
            dma((NY - 1, PAIRS)), dma((NY - 1, PAIRS)), dma((NZ,)), dma((NZ,)),
            dma((2,)), dma((2,)), dma((2, NZ)), dma((2, NZ)), dma((NZ,)), dma((NZ,)), dma((1,)), dma((1,)),
        ],
        compiler_params=pltpu.CompilerParams(
            collective_id=0, has_side_effects=True, vmem_limit_bytes=60 * 1024 * 1024
        ),
        cost_estimate=pl.CostEstimate(flops=9_000_000_000, bytes_accessed=14_000_000, transcendentals=8_000_000),
        name="layer_grad",
    )(*args)
    return pl.pallas_call(
        copy_kernel,
        out_shape=out_shape,
        in_specs=[whole] * 4,
        out_specs=[whole] * 4,
        name="hand_out",
    )(*grads)


def solution(mesh):
    return jax.shard_map(
        on_device,
        mesh=mesh,
        in_specs=(
            P("expert", "pipe"),
            P("expert", None),
            P("expert", None),
            P("expert", None),
            P("expert", None, None),
            P("expert", None, None),
            P("expert", "pipe", None),
            P("expert", "pipe", None),
            P("expert", None, "pipe"),
            P("expert", "pipe"),
            P("expert", "pipe"),
            P("expert", "pipe"),
            P("expert", "pipe"),
            P("expert", "pipe"),
        ),
        out_specs=(
            P("expert", "pipe"),
            P("expert", "pipe"),
            P("expert", "pipe"),
            P("expert", "pipe"),
        ),
        check_vma=False,
    )
```

time: 158 us -> 103 us (0.65)
  the two profiles are of different devices: /device:TPU:8 before, /device:TPU:17 now
where the time goes in v2:
time: 103 us
  Pallas kernels  102 us (99%)
    pallas_call x1, Pallas kernels, on_device(): pl.pallas_call(kernel, out_shape=out_shape, in_specs=[whole] * 4 + [anywh...  101 us

profile of v2, /device:TPU:17, one launch (start us, length us, event | category | flops | bytes accessed | tf_op | source)
XLA Modules:
  0.0 103.1 jit_solution(8603850700084769482)
XLA Ops:
  0.6 100.8 %layer_grad.1 = (bf16[32,768]{1,0:T(8,128)(2,1)}, bf16[128,768]{1,0:T(8,128)(2,1)}, bf16[128,128]{1,0:T(8,128)(2,1)}, bf16[128,128]{1,0:T(8,128)(2,1)}) custom-call(bf16[32,768]{1,0:T(8,128)(2,1)} %upper_ref.1, s32[4,32]{1,0:T(4,128)} %bitcast.11, s32[4,32]{1,0:T(4,128)} %bitcast.12, f32[4,32]{1,0:T(4,128)} %bitcast.13, bf16[1,1344,768]{2,1,0:T(8,128)(2,1)} %bitcast.7, ...), custom_call_target="tpu_custom_call" | custom-call | flops 8999999488 | bytes 14000000 | tf_op jit(solution)/shard_map/layer_grad/pallas_call | solution.py:691
  101.4 1.7 %hand_out.1 = (bf16[32,768]{1,0:T(8,128)(2,1)}, bf16[128,768]{1,0:T(8,128)(2,1)}, bf16[128,128]{1,0:T(8,128)(2,1)}, bf16[128,128]{1,0:T(8,128)(2,1)}) custom-call(bf16[32,768]{1,0:T(8,128)(2,1)} %get-tuple-element.8.refs_0_, bf16[128,768]{1,0:T(8,128)(2,1)} %get-tuple-element.9.refs_1_, bf16[128,128]{1,0:T(8,128)(2,1)} %get-tuple-element.10.refs_2_, ...), custom_call_target="tpu_custom_call" | custom-call | tf_op jit(solution)/shard_map/hand_out/pallas_call | solution.py:724

commit v3 on v2

--- a/solution.py
+++ b/solution.py
@@ -1,3 +1,5 @@
+import math
+
 import jax
 import jax.numpy as jnp
 from jax import lax
@@ -24,8 +26,10 @@
 PAIR_SLOTS = 2 * CAP
 ROW_SLOTS = NZ * CAP
 KEYS = 2 * ATT
+WIDE = 2
 BLOCKS = NY * PAIRS
 SCALE = HEAD_DIM ** (-0.5)
+SCALE_BITS = SCALE * math.log2(math.e)
 MASKED = -1e30
 
 NT = (((1,), (1,)), ((), ()))
@@ -84,15 +88,13 @@
             )
         )
     ]
-    for n in (5, 6, 1, 2, 0, 7, 9, 8, 3, 4):
-        loads[n].start()
 
     upg[z] = upper_ref[...]
     kept = slot_ref[...] >= 0
     dtmp[...] = jnp.zeros((ATT, 256), F32)
     dtmp[0:4, 0:TOK] = jnp.where(kept, ids_ref[...] * CAP + slot_ref[...], -1).astype(F32)
     dtmp[4:8, 0:TOK] = prob_ref[...]
-    metag[z] = dtmp[:, 0:128].T[0:TOK]
+    metag[z] = dtmp[0:8, 0:128]
 
     barrier = pltpu.get_barrier_semaphore()
     peers = (
@@ -214,18 +216,18 @@
 
         lax.fori_loop(0, NZ, kv_forward, 0)
 
-    def score_block(b, masked):
-        keys = kg[pl.ds(2 * b, 2)].reshape(KEYS, 128)
-        s = dot(keys, qrows[...], NT) * SCALE
+    def score_block(b, count, masked):
+        keys = kg[pl.ds(2 * b, 2 * count)].reshape(count * KEYS, 128)
+        s = dot(keys, qrows[...], NT) * SCALE_BITS
         if masked:
             key_pos = b * KEYS + lax.broadcasted_iota(jnp.int32, (KEYS, ROWS), 0)
             row_pos = e * ATT + (lax.broadcasted_iota(jnp.int32, (KEYS, ROWS), 1) & 127)
             s = jnp.where(key_pos <= row_pos, s, MASKED)
-        scores[b] = s
-        mrun[...] = jnp.maximum(mrun[...], jnp.max(s.reshape(KEYS // 8, 8, ROWS), axis=0))
+        scores[pl.ds(b, count)] = s.reshape(count, KEYS, ROWS)
+        mrun[...] = jnp.maximum(mrun[...], jnp.max(s.reshape(count * KEYS // 8, 8, ROWS), axis=0))
 
     def score_step(b, carry):
-        score_block(b, False)
+        score_block(b, 1, False)
         return carry
 
     last = e // 2
@@ -266,15 +268,18 @@
             def _():
                 t_copy(n, rel).start()
 
-    def grad_block(b):
-        keys = kg[pl.ds(2 * b, 2)].reshape(KEYS, 128)
-        values = vg[pl.ds(2 * b, 2)].reshape(KEYS, 128)
-        probs = jnp.exp(scores[b] - stat[...])
+    def grad_block(b, count):
+        size = count * KEYS
+        keys = kg[pl.ds(2 * b, 2 * count)].reshape(size, 128)
+        values = vg[pl.ds(2 * b, 2 * count)].reshape(size, 128)
+        probs = jnp.exp2(scores[pl.ds(b, count)].reshape(size, ROWS) - stat[...])
         grad_probs = dot(values, dorows[...], NT)
-        ds = (probs * (grad_probs - delta[...]) * SCALE).astype(BF16)
+        ds = (probs * (grad_probs - delta[...])).astype(BF16)
         dqt[...] += dot(keys, ds, TN)
-        dkv[pl.ds(2 * b, 2), :, 0:128] = dot(ds, qrows[...], NN).astype(BF16).reshape(2, ATT, 128)
-        dkv[pl.ds(2 * b, 2), :, 128:256] = dot(probs.astype(BF16), dorows[...], NN).astype(BF16).reshape(2, ATT, 128)
+        key_grad = (dot(ds, qrows[...], NN) * SCALE).astype(BF16)
+        value_grad = dot(probs.astype(BF16), dorows[...], NN).astype(BF16)
+        dkv[pl.ds(2 * b, 2 * count), :, 0:128] = key_grad.reshape(2 * count, ATT, 128)
+        dkv[pl.ds(2 * b, 2 * count), :, 128:256] = value_grad.reshape(2 * count, ATT, 128)
 
     def dy_copy(yrel, ydst, blk):
         src = dkv.at[pl.ds(ydst * NZ + 2 * blk, 2)]
@@ -352,8 +357,8 @@
             prod = do_ref[:, cols].astype(F32) * o_ref[:, cols].astype(F32)
             delta[:, cols] = jnp.sum(prod.T, axis=0, keepdims=True)
 
-    def dispatch():
-        for j in (0, 1, 3, 2):
+    def dispatch(turns):
+        for j in turns:
             pair = (z // 2 + j) % PAIRS
             for i in range(2):
                 zz = pair * 2 + i
@@ -363,7 +368,7 @@
                     up_copy(zz, z).wait_recv()
                     meta_copy(zz, z).wait_recv()
 
-                meta = metag[zz]
+                meta = metag[zz].T[0:TOK]
                 tokens = upg[zz].astype(F32)
                 target = meta[:, 0:4].astype(jnp.int32)
                 mine = jnp.where(col_i == i, wanted, -2)
@@ -385,7 +390,7 @@
 
     def own_scores():
         mrun[...] = jnp.full((8, ROWS), MASKED, F32)
-        score_block(last, True)
+        score_block(last, 1, True)
         lax.fori_loop(y * PAIRS, last, score_step, 0)
 
     def row_scores(yrel):
@@ -401,18 +406,23 @@
                 kv2_wait(0)
             else:
                 lax.fori_loop(0, NZ, k_wait, 0)
-            lax.fori_loop(ysrc * PAIRS, ysrc * PAIRS + PAIRS, score_step, 0)
+
+            def wide_step(i, carry):
+                score_block(ysrc * PAIRS + WIDE * i, WIDE, False)
+                return carry
+
+            lax.fori_loop(0, PAIRS // WIDE, wide_step, 0)
 
     def totals():
         top = jnp.max(mrun[...], axis=0, keepdims=True)
         lrun[...] = jnp.zeros((8, ROWS), F32)
 
         def sum_step(b, carry):
-            lrun[...] += jnp.sum(jnp.exp(scores[b] - top).reshape(KEYS // 8, 8, ROWS), axis=0)
+            lrun[...] += jnp.sum(jnp.exp2(scores[b] - top).reshape(KEYS // 8, 8, ROWS), axis=0)
             return carry
 
         lax.fori_loop(0, last + 1, sum_step, 0)
-        stat[...] = top + jnp.log(jnp.sum(lrun[...], axis=0, keepdims=True))
+        stat[...] = top + jnp.log2(jnp.sum(lrun[...], axis=0, keepdims=True))
         dqt[...] = jnp.zeros((128, ROWS), F32)
 
     def gather_hidden(h):
@@ -448,21 +458,22 @@
                 lax.fori_loop(0, NZ, v_wait, 0)
 
             def row_step(turn, carry):
-                blk = (z // 2 + 1 + turn) % PAIRS
-                grad_block((y - yrel) * PAIRS + blk)
-                if yrel == 2:
-                    for i in range(2):
-                        zz = 2 * blk + i
-
-                        @pl.when(zz != z)
-                        def _():
-                            d2z_copy(z, zz).start()
-
-                else:
-                    dy_copy(yrel, y - yrel, blk).start()
+                first = (z // 2 + WIDE * (turn + 1)) % PAIRS // WIDE * WIDE
+                grad_block((y - yrel) * PAIRS + first, WIDE)
+                for i in range(WIDE):
+                    if yrel == 2:
+                        for j in range(2):
+                            zz = 2 * (first + i) + j
+
+                            @pl.when(zz != z)
+                            def _():
+                                d2z_copy(z, zz).start()
+
+                    else:
+                        dy_copy(yrel, y - yrel, first + i).start()
                 return carry
 
-            lax.fori_loop(0, PAIRS, row_step, 0)
+            lax.fori_loop(0, PAIRS // WIDE, row_step, 0)
 
     def combine(n):
         for yrel in y_order:
@@ -493,7 +504,7 @@
 
             @pl.when(b <= last)
             def _():
-                grad_block(b)
+                grad_block(b, 1)
 
             @pl.when(b > last)
             def _():
@@ -504,7 +515,7 @@
         lax.fori_loop(0, PAIRS, own_step, 0)
         for g in range(GROUP):
             cols = slice(g * 128, (g + 1) * 128)
-            dq_ref[:, cols] = dqt[:, cols].T.astype(BF16)
+            dq_ref[:, cols] = (dqt[:, cols].T * SCALE).astype(BF16)
 
     def dz_copy(zsrc, zdst):
         return remote(dzsend.at[zdst], dzrecv.at[zsrc], dz_s.at[zdst], dz_r.at[zsrc], z_dev(zdst))
@@ -543,8 +554,13 @@
         lax.fori_loop(0, PAIRS, pair_step, 0)
         down[...] = dtmp[...]
 
+    def start(*which):
+        for n in which:
+            loads[n].start()
+
+    start(5, 6, 1, 2, 0, 7, 9, 8, 3, 4)
     turn_gate()
-    dispatch()
+    dispatch((0, 1, 3, 2))
     for n in (5, 6):
         loads[n].wait()
     send_kv()
@@ -696,7 +712,7 @@
         scratch_shapes=[
             vmem(COLS, UNITS), vmem(COLS, UNITS), vmem(UNITS, COLS), vmem(UNITS, COLS),
             vmem(UNITS, COLS), vmem(UNITS, COLS), vmem(UNITS, COLS), vmem(ATT, COLS), vmem(ATT, COLS), vmem(ATT, COLS), dma((10,)),
-            vmem(NZ, TOK, COLS), vmem(NZ, TOK, 128, dtype=F32), vmem(8 * TOK, COLS), vmem(8 * TOK, ROW_SLOTS),
+            vmem(NZ, TOK, COLS), vmem(NZ, 8, 128, dtype=F32), vmem(8 * TOK, COLS), vmem(8 * TOK, ROW_SLOTS),
             vmem(PAIRS, 2 * TOK, ROW_SLOTS), vmem(NY, ROW_SLOTS, COLS), vmem(NY, ROW_SLOTS, COLS),
             vmem(2, ROW_SLOTS, UNITS, dtype=F32), vmem(2, ROW_SLOTS, UNITS), vmem(2, ROW_SLOTS, UNITS),
             vmem(2, NX, PAIR_SLOTS, UNITS), vmem(2, NX - 1, PAIR_SLOTS, UNITS), vmem(2, PAIR_SLOTS, UNITS, dtype=F32),

time: 103 us -> 102 us (level)
    pallas_call x1, Pallas kernels: 101 us -> 98.9 us  [on_device(): pl.pallas_call(kernel, out_shape=out_shape, in_specs=[whole] * 4 + [anywh...]
where the time goes in v3:
time: 102 us; the launch traced here: 101 us
  Pallas kernels  101 us (99%)
    pallas_call x1, Pallas kernels, on_device(): pl.pallas_call(kernel, out_shape=out_shape, in_specs=[whole] * 4 + [anywh...  98.9 us

profile of v3, /device:TPU:17, one launch (start us, length us, event | category | flops | bytes accessed | tf_op | source)
XLA Modules:
  0.0 101.2 jit_solution(190779753650105272)
XLA Ops:
  0.6 98.9 %layer_grad.1 = (bf16[32,768]{1,0:T(8,128)(2,1)}, bf16[128,768]{1,0:T(8,128)(2,1)}, bf16[128,128]{1,0:T(8,128)(2,1)}, bf16[128,128]{1,0:T(8,128)(2,1)}) custom-call(bf16[32,768]{1,0:T(8,128)(2,1)} %upper_ref.1, s32[4,32]{1,0:T(4,128)} %bitcast.11, s32[4,32]{1,0:T(4,128)} %bitcast.12, f32[4,32]{1,0:T(4,128)} %bitcast.13, bf16[1,1344,768]{2,1,0:T(8,128)(2,1)} %bitcast.7, ...), custom_call_target="tpu_custom_call" | custom-call | flops 8999999488 | bytes 14000000 | tf_op jit(solution)/shard_map/layer_grad/pallas_call | solution.py:707
  99.6 1.7 %hand_out.1 = (bf16[32,768]{1,0:T(8,128)(2,1)}, bf16[128,768]{1,0:T(8,128)(2,1)}, bf16[128,128]{1,0:T(8,128)(2,1)}, bf16[128,128]{1,0:T(8,128)(2,1)}) custom-call(bf16[32,768]{1,0:T(8,128)(2,1)} %get-tuple-element.8.refs_0_, bf16[128,768]{1,0:T(8,128)(2,1)} %get-tuple-element.9.refs_1_, bf16[128,128]{1,0:T(8,128)(2,1)} %get-tuple-element.10.refs_2_, ...), custom_call_target="tpu_custom_call" | custom-call | tf_op jit(solution)/shard_map/hand_out/pallas_call | solution.py:740
